TPU v7x, 32 devices: a whole 2x2x4 slice. The times are simulated.
32 devices in a mesh: edge: 16 (over z, y, x), rep: 2 (over core).
Axes of the slice: x: 2, y: 2, z: 4, core: 2. Of those that a mesh axis runs over, the one named last changes fastest.
Arguments:
- node_feat: float32 [2, 8192, 14], P('rep', 'edge'), may hold values from -6 to 6
- node_types: int32 [2, 8192], P('rep', 'edge'), may hold values from 0 to 8
- boundary: int32 [2, 8192], P('rep', 'edge'), may hold values from 0 to 1
- target: float32 [2, 8192, 2], P('rep', 'edge'), may hold values from -6 to 6
- edge_feat: float32 [2, 131072, 3], P('rep', 'edge'), may hold values from -6 to 6
- senders: int32 [2, 131072], P('rep', 'edge'), may hold values from 0 to 8191, as said below
- receivers: int32 [2, 131072], P('rep', 'edge'), may hold values from 0 to 8191, as said below
- edge_counts: int32 [2, 16], P('rep', 'edge'), may hold values from 4096 to 8192, as said below
- mats: float32 [24, 128, 128], replicated, may hold values from -0.5 to 0.5
- vecs: float32 [60, 128], replicated
- mats_momentum: float32 [24, 128, 128], replicated, may hold values from -0.25 to 0.25
- vecs_momentum: float32 [60, 128], replicated, may hold values from -0.25 to 0.25
- factors: float32 [24, 128, 8], replicated, may hold values from -6 to 6
- errors: float32 [2, 24, 128, 128], P('rep'), may hold values from -0.25 to 0.25
Outputs:
- loss_sum: float32 [], replicated
- loss_count: float32 [], replicated
- stats: float32 [4, 2], replicated
- new_mats: float32 [24, 128, 128], replicated
- new_mats_momentum: float32 [24, 128, 128], replicated
- new_factors: float32 [24, 128, 8], replicated
- new_errors: float32 [2, 24, 128, 128], P('rep')
- new_vecs: float32 [60, 128], replicated
- new_vecs_momentum: float32 [60, 128], replicated
Inputs may be any that keep to these rules, and one draw needn't show every extreme that they name: `edge_counts`: multiples of 128; the live slots of a device come first; in each scene some device has all 8192 slots live. `receivers`: every edge slot of device d of a scene has its receiver among the particles d * 512 to (d + 1) * 512 - 1. `senders`: each sender lies within 512 particles of its edge's receiver.
All inputs are finite; a program needn't handle non-finite values.
Results may differ from a plain program's by a relative error of at most 0.0003.
Values sent between devices are 32-bit elements; how exact they have to be, the bound alone decides.
A program may use at most 256 MiB of HBM per device.

v0:
```python
from functools import partial

import jax
import jax.numpy as jnp
from jax import lax
from jax.experimental import pallas as pl
from jax.experimental.pallas import tpu as pltpu
from jax.sharding import PartitionSpec as P

NFEAT = 14
NTYPES = 9
EFEAT = 3
LEAD = NFEAT + NTYPES
ROWS0 = LEAD + EFEAT
LAT = 128
BLOCK = 2048
SUB = 512
SHIFT = 10
NONE = (1 << SHIFT) - 1
F32 = jnp.float32
BF16 = jnp.bfloat16
MESH = pl.DeviceIdType.MESH
NN = (((1,), (0,)), ((), ()))
NT = (((1,), (1,)), ((), ()))
TN = (((0,), (0,)), ((), ()))


def mm(a, b, dims=NN):
    return lax.dot_general(a, b, dims, preferred_element_type=F32)


def split(w):
    hi = w.astype(BF16)
    return hi, (w - hi.astype(F32)).astype(BF16)


def twice(a):
    return jnp.concatenate([a, a], 1)


def stacked(w):
    return jnp.concatenate(split(w), 0)


def side_by_side(v):
    return jnp.concatenate(split(v), 1)


def joined(wide):
    return wide[:, :LAT] + wide[:, LAT:]


def mm3(a, b, dims=NN):
    ah, al = split(a)
    bh, bl = split(b)
    (axis_a,), (axis_b,) = dims[0]
    if a.shape[axis_a] % LAT:
        return mm(ah, bh, dims) + (mm(ah, bl, dims) + mm(al, bh, dims))
    a = jnp.concatenate([ah, ah, al], axis_a)
    return mm(a, jnp.concatenate([bh, bl, bh], axis_b), dims)


def silu_half(half):
    rest = jnp.tanh(half)
    up = 1.0 + rest
    value = half * up
    return value, up + value * (1.0 - rest)


def mean_last(v):
    return jnp.mean(v, -1, keepdims=True)


def center(w):
    return w - mean_last(w)


def fold_rows(v):
    total = v[0:8]
    for i in range(8, v.shape[0], 8):
        total = total + v[i : i + 8]
    return total


def row_sum(v):
    return jnp.sum(fold_rows(v), 0, keepdims=True)


def fold_table(v):
    half = v.shape[0] // 2
    return jnp.concatenate([v[:half], v[half:]], 1).astype(BF16)


def unfold(v):
    return jnp.concatenate([v[:, :LAT], v[:, LAT:]], 0)


def together(parts):
    parts = list(parts)
    while parts:
        for part in list(parts):
            try:
                next(part)
            except StopIteration:
                parts.remove(part)


def node_tail(first, second, third, vec):
    b1, b2, b3, g, o = vec
    half1 = 0.5 * (first + b1)
    half2 = 0.5 * (mm3(silu_half(half1)[0], second) + b2)
    z = mm3(silu_half(half2)[0], third) + b3
    c = z - mean_last(z)
    inv = lax.rsqrt(mean_last(c * c) + 1e-05)
    xhat = c * inv
    return xhat * g + o, (half1, half2, xhat, jnp.broadcast_to(inv, xhat.shape))


def node_tail_back(d, kept, second, third, vec):
    half1, half2, xhat, inv = kept
    s1, d1 = silu_half(half1)
    s2, d2 = silu_half(half2)
    dy = d * vec[3]
    dz3 = inv * (dy - mean_last(dy) - xhat * mean_last(dy * xhat))
    dz2 = mm3(dz3, 0.5 * third, NT) * d2
    dz1 = mm3(dz2, 0.5 * second, NT) * d1
    rows = [row_sum(v) for v in (dz1, dz2, dz3, d * xhat, d)]
    return dz1, mm3(s1, dz2, TN), mm3(s2, dz3, TN), rows


def edge_tail(rows, half, kept, second, third, vec, ones):
    _, b2, b3, g, o = vec
    kept[0][rows, :] = half.astype(BF16)
    s1 = silu_half(half)[0].astype(BF16)
    half = mm(twice(s1), second) + 0.5 * b2
    yield
    kept[1][rows, :] = half.astype(BF16)
    s2 = silu_half(half)[0].astype(BF16)
    c = mm(twice(s2), third) + center(b3)
    yield
    inv = lax.rsqrt(mm((c * c).astype(BF16), ones) + 1e-05)
    xhat = c * inv
    kept[2][rows, :] = xhat.astype(BF16)
    kept[3][rows, :] = inv.astype(BF16)
    return xhat * g + o


def edge_tail_back(rows, d, kept, second, third, g, ones, sums):
    xhat = kept[2][rows, :].astype(F32)
    inv = kept[3][rows, :].astype(F32)
    dx = d * xhat
    dc = inv * (d * g - xhat * mm((dx * g).astype(BF16), ones))
    dcb = dc.astype(BF16)
    for at, v in ((2, dc), (3, dx), (4, d)):
        sums[at] += fold_rows(v)
    yield
    s2, d2 = silu_half(kept[1][rows, :].astype(F32))
    dz2 = mm(twice(dcb), third) * d2
    sums[1] += fold_rows(dz2)
    dz2b = dz2.astype(BF16)
    yield
    s1, d1 = silu_half(kept[0][rows, :].astype(F32))
    dz1 = mm(twice(dz2b), second) * d1
    sums[0] += fold_rows(dz1)
    return dz1, dz2b, dcb, s1.astype(BF16), s2.astype(BF16)


def finish_sums(sums):
    rows = [jnp.sum(sums[i], 0, keepdims=True) for i in range(5)]
    rows[2] = center(rows[2])
    return rows


def columns_of(code):
    parts = [
        jnp.transpose(jnp.broadcast_to(code[q : q + 1, :], (LAT, LAT))) for q in range(code.shape[0])
    ]
    return jnp.concatenate(parts, 0)


def pick_mask(column, begin, count):
    lanes = lax.broadcasted_iota(jnp.int32, (column.shape[0], LAT), 1)
    parts = [
        jnp.where(column == lanes + at, 1.0, 0.0).astype(BF16)
        for at in range(begin, begin + count, LAT)
    ]
    return jnp.concatenate(parts, 1)


def add_mask(row, count):
    down = lax.broadcasted_iota(jnp.int32, (count, LAT), 0)
    parts = [
        jnp.where(row[q : q + 1, :] == down, 1.0, 0.0).astype(BF16) for q in range(row.shape[0])
    ]
    return jnp.concatenate(parts, 1)


def halves(v, upper):
    return jnp.concatenate([jnp.where(upper, 0.0, v), jnp.where(upper, v, 0.0)], 1).astype(BF16)


def choose(wide, upper):
    return jnp.where(upper, wide[:, LAT:], wide[:, :LAT])


def encode_pairs(send, recv, live, own):
    half = own // 2
    inner = (send >= own) & (send < 2 * own)
    upper = (send >= 2 * own) | (inner & (send >= own + half))
    at = jnp.where(inner, send - own, jnp.where(upper, send - 2 * own, send) + half)
    at = jnp.where(inner & upper, at - half, at)
    code = (at << SHIFT) + recv
    code = jnp.where(upper, code + -(1 << 31), code)
    return jnp.where(live, code, (NONE << SHIFT) + NONE)


def send_of(code):
    return (code >> SHIFT) & NONE


def recv_of(code):
    return code & NONE


def upper_of(code):
    return code < 0


def folded(index, half):
    return jnp.where(index >= half, index - half, index)


def orders_of(count):
    if count == 16:
        near, far = (4, 1), (4, 4)
        return [[near, far], [far, near]]
    if count == 64:
        a, b, c = (4, 1), (4, 4), (4, 16)
        return [[a, b, c], [b, c, a]]
    return [[(count, 1)], [(count, 1)]]


class Reducer:
    def __init__(self, count, rows):
        self.orders = orders_of(count)
        unit = 8 * count
        units = max(-(-rows // unit), 2)
        self.rows = units * unit
        near = min(max(round(units * 2 / 3), 1), units - 1) * unit
        self.parts = ((0, near), (near, self.rows - near))
        stages = len(self.orders[0])
        self.sequence = [(i, 0) for i in range(stages)] + [(i, 1) for i in reversed(range(stages))]
        self.steps = len(self.sequence) + 1

    def scratch(self):
        shapes = {"acc": pltpu.VMEM((self.rows, LAT), F32), "full": pltpu.VMEM((self.rows, LAT), F32)}
        copies = 0
        for half, order in enumerate(self.orders):
            length = self.parts[half][1]
            for stage, (k, _) in enumerate(order):
                length //= k
                shapes[f"slot{half}{stage}"] = pltpu.VMEM((max(k - 1, 1), length, LAT), F32)
                copies += k - 1
        shapes["send"] = pltpu.SemaphoreType.DMA((2 * copies,))
        shapes["recv"] = pltpu.SemaphoreType.DMA((2 * copies,))
        return shapes

    def bind(self, refs):
        self.refs = refs
        self.acc, self.full = refs["acc"], refs["full"]
        me = lax.axis_index("edge")
        self.begin = []
        self.length = []
        self.sems = {}
        used = 0
        for half, order in enumerate(self.orders):
            begin = [self.parts[half][0]]
            length = [self.parts[half][1]]
            for k, stride in order:
                length.append(length[-1] // k)
                begin.append(begin[-1] + ((me // stride) % k) * length[-1])
            self.begin.append(begin)
            self.length.append(length)
            for stage, (k, stride) in enumerate(order):
                for t in range(1, k):
                    for phase in range(2):
                        mine = (me // stride) % k
                        other = (mine + t) % k
                        self.sems[half, stage, phase, t] = (used, other, me + (other - mine) * stride)
                        used += 1

    def peers(self):
        order = self.orders[0]
        return [
            self.sems[0, stage, 0, t][2]
            for stage in range(len(order))
            for t in range(1, order[stage][0])
        ]

    def window(self, begin, length):
        return pl.ds(pl.multiple_of(begin, 8), length)

    def copies(self, half, stage, phase):
        k = self.orders[half][stage][0]
        out = []
        for t in range(1, k):
            at, other, device = self.sems[half, stage, phase, t]
            length = self.length[half][stage + 1]
            if phase == 0:
                rows = self.window(self.begin[half][stage] + other * length, length)
                source, target = self.acc.at[rows], self.refs[f"slot{half}{stage}"].at[t - 1]
            else:
                rows = self.window(self.begin[half][stage + 1], length)
                source = target = self.full.at[rows]
            out.append(
                pltpu.make_async_remote_copy(
                    src_ref=source,
                    dst_ref=target,
                    send_sem=self.refs["send"].at[at],
                    recv_sem=self.refs["recv"].at[at],
                    device_id={"edge": device},
                    device_id_type=MESH,
                )
            )
        return out

    def start(self, half, stage, phase):
        for one in self.copies(half, stage, phase):
            one.start()

    def wait(self, half, stage, phase):
        for one in self.copies(half, stage, phase):
            one.wait()
        if phase:
            return
        rows = self.window(self.begin[half][stage + 1], self.length[half][stage + 1])
        value = self.acc[rows, :]
        for t in range(1, self.orders[half][stage][0]):
            value = value + self.refs[f"slot{half}{stage}"][t - 1]
        if stage == len(self.orders[half]) - 1:
            self.full[rows, :] = value
        else:
            self.acc[rows, :] = value

    def step(self, index):
        for half in range(2):
            if index:
                self.wait(half, *self.sequence[index - 1])
            if index < len(self.sequence):
                self.start(half, *self.sequence[index])


PLACES = (
    (4, 5, 20, 21, 22, 23),
    (15, 18, 19, 16, 17, 11, 12, 13, 14),
    (6, 9, 10, 7, 8, 0, 1),
    (2, 3),
)
ROWS = (32, 8, 48, 8)
STARTS = tuple(sum(ROWS[:i]) for i in range(5))


class Refs(dict):
    def __getattr__(self, name):
        return self[name]


def train_kernel(reducers, names, mats_count, rank, *refs):
    r = Refs(zip(names, refs))
    groups = []
    for i, reducer in enumerate(reducers):
        mark = f"sum{i}_"
        reducer.bind({k[len(mark) :]: v for k, v in r.items() if k.startswith(mark)})
        groups.append(reducer)
    first, second, third, fourth = groups
    own = r.goal.shape[1]
    count = r.code.shape[0] * LAT
    lines = own // LAT
    me = lax.axis_index("edge")
    last = lax.axis_size("edge") - 1
    has_left, has_right = me > 0, me < last
    sibling = {"rep": 1 - lax.axis_index("rep")}
    barrier = pltpu.get_barrier_semaphore()
    around = [lax.rem(me + shift, last + 1) for shift in (1, last)]
    others = [{"edge": one} for one in first.peers() + around] + [sibling]
    for peer in others:
        pl.semaphore_signal(barrier, inc=1, device_id=peer, device_id_type=MESH)
    fetches = [
        pltpu.make_async_copy(source, target, r.fetch_sem.at[at])
        for at, (source, target) in enumerate(
            (
                (r.mats_in.at[pl.ds(2, 2)], r.mats.at[pl.ds(2, 2)]),
                (r.mats_in.at[pl.ds(0, 2)], r.mats.at[pl.ds(0, 2)]),
                (r.mats_in.at[pl.ds(4, mats_count - 4)], r.mats.at[pl.ds(4, mats_count - 4)]),
                (r.errors_in, r.errors),
            )
        )
    ]
    for one in fetches:
        one.start()
    mats, vecs = r.mats, r.vecs
    ones = jnp.full((LAT, LAT), 1.0 / LAT, BF16)
    middle = pl.ds(own, own)
    r["spread"] = r.hb
    r["agg_wide"] = r.recv_total

    def rows_of(which):
        base = ROWS0 + 5 * which
        return [vecs[base + i : base + i + 1, :] for i in range(5)]

    for q in range(lines):
        lanes = slice(q * LAT, (q + 1) * LAT)
        r.feat_wide[1, 0:NFEAT, lanes] = r.node_lines[pl.ds(q, NFEAT, stride=lines), :]
        r.feat_wide[1, NFEAT : NFEAT + 1, lanes] = r.types[q : q + 1, :].astype(F32)
        r.keep[:, lanes] = (1 - r.boundary[q : q + 1, :]).astype(F32)
    r.feat_wide[1, NFEAT + 1 :, :] = jnp.zeros((1, own), F32)

    @pl.when(me == 0)
    def _():
        r.feat_wide[0] = jnp.zeros(r.feat_wide.shape[1:], F32)
        r.hb[0:own, :] = jnp.zeros((own, LAT), F32)
        r.rims[0] = jnp.zeros((own, LAT), F32)

    @pl.when(me == last)
    def _():
        r.feat_wide[2] = jnp.zeros(r.feat_wide.shape[1:], F32)
        r.hb[2 * own :, :] = jnp.zeros((own, LAT), F32)
        r.rims[1] = jnp.zeros((own, LAT), F32)

    slots = lax.broadcasted_iota(jnp.int32, r.code.shape, 0) * LAT
    slots = slots + lax.broadcasted_iota(jnp.int32, r.code.shape, 1)
    send = r.senders[...] - (me - 1) * own
    r.code[...] = encode_pairs(send, r.receivers[...] - me * own, slots < r.counts[...], own)

    def neighbours(at, up, up_target, down, down_target):
        def one(index, source, target, shift):
            return pltpu.make_async_remote_copy(
                src_ref=source,
                dst_ref=target,
                send_sem=r.halo_send.at[at + index],
                recv_sem=r.halo_recv.at[at + index],
                device_id={"edge": me + shift},
                device_id_type=MESH,
            )

        return one(0, up, up_target, 1), one(1, down, down_target, -1)

    def start(pair):
        @pl.when(has_right)
        def _():
            pair[0].start()

        @pl.when(has_left)
        def _():
            pair[1].start()

    def wait(pair):
        @pl.when(has_right)
        def _():
            pair[0].wait_send()
            pair[1].wait_recv()

        @pl.when(has_left)
        def _():
            pair[1].wait_send()
            pair[0].wait_recv()

    mine = r.feat_wide.at[1]
    feats = neighbours(0, mine, r.feat_wide.at[0], mine, r.feat_wide.at[2])

    def begin():
        pl.semaphore_wait(barrier, len(others))
        start(feats)

    turns = count // BLOCK

    def steps_of(group):
        return {index: partial(group.step, index) for index in range(turns)}

    def loop(body, hooks=None):
        def step(i, unused):
            for index, hook in (hooks or {}).items():
                pl.when(i == index)(hook)

            base = pl.multiple_of(i * (BLOCK // LAT), BLOCK // LAT)
            code = r.code[pl.ds(base, BLOCK // LAT), :]
            per = count // LAT
            planes = [r.x[pl.ds(base + p * per, BLOCK // LAT), :] for p in range(EFEAT)]
            parts = []
            for at in range(0, BLOCK, SUB):
                rows = pl.ds(pl.multiple_of(i * BLOCK + at, SUB), SUB)
                cut = slice(at // LAT, (at + SUB) // LAT)
                parts.append(body(rows, code[cut], [plane[cut] for plane in planes]))
            together(parts)
            return unused

        lax.fori_loop(0, count // BLOCK, step, 0)

    def features(planes):
        lines = [
            jnp.concatenate([plane[q : q + 1, :] for q in range(plane.shape[0])], 1)
            for plane in planes
        ]
        return jnp.concatenate(lines, 0)

    kept = [[r[f"{name}{i}"] for i in range(4)] for name in ("enc", "one", "two")]

    fetches[0].wait()
    r.w[0] = stacked(0.5 * mats[2])
    r.w[1] = stacked(center(mats[3]))
    vec = rows_of(1)

    def encode(rows, code, planes):
        half = mm3(features(planes), 0.5 * vecs[LEAD:ROWS0, :], TN) + 0.5 * vec[0]
        yield
        out = yield from edge_tail(rows, half, kept[0], r.w[0], r.w[1], vec, ones)
        r.e0[rows, :] = out.astype(BF16)

    loop(encode, {turns // 2: begin})

    fetches[1].wait()
    fetches[2].wait()
    wait(feats)
    def particle_inputs():
        values = jnp.concatenate([r.feat_wide[i] for i in range(3)], 1)
        types = lax.broadcasted_iota(jnp.int32, (NTYPES, 3 * own), 0).astype(F32)
        return values[0:NFEAT], jnp.where(values[NFEAT : NFEAT + 1] == types, 1.0, 0.0)

    plain, onehot = particle_inputs()
    pre = mm3(plain, vecs[0:NFEAT, :], TN) + mm3(onehot, vecs[NFEAT:LEAD, :], TN)
    out, saved = node_tail(pre, mats[0], mats[1], rows_of(0))
    r.h0[...] = out
    for j, v in enumerate(saved):
        r.node_kept[j] = v
    latent = 0.5 * mm3(out, mats[7])
    half = own // 2

    def put_inner(v):
        r.senders_table[0:half, :] = jnp.concatenate([v[:half], v[half:]], 1).astype(BF16)

    def put_outer(left, right):
        r.senders_table[half:, :] = jnp.concatenate([left, right], 1).astype(BF16)

    put_inner(latent[own : 2 * own])
    put_outer(latent[:own], latent[2 * own :])
    shared = rows_of(2)[0]
    r.recv_table[...] = side_by_side(0.5 * (mm3(out[own : 2 * own], mats[8]) + shared))

    def put_weights(step):
        base = 6 + 9 * step
        r.w[0] = stacked(0.5 * mats[base])
        r.w[1] = stacked(0.5 * mats[base + 3])
        r.w[2] = stacked(center(mats[base + 4]))

    def near_part(column, e):
        wide = mm(pick_mask(recv_of(column), 0, own), r.recv_table[...])
        return joined(wide) + mm(twice(e), r.w[0])

    def sent_part(column, begin, end):
        wide = mm(pick_mask(send_of(column), begin, end - begin), r.senders_table[begin:end, :])
        return choose(wide, upper_of(column))

    def add_up(rows, half1, code, column, step, vec):
        out = yield from edge_tail(rows, half1, kept[1 + step], r.w[1], r.w[2], vec, ones)
        r.agg_wide[...] += mm(
            add_mask(folded(recv_of(code), half), half), halves(out, recv_of(column) >= half)
        )
        return out

    put_weights(0)
    r.agg_wide[...] = jnp.zeros_like(r.agg_wide)
    vec0 = rows_of(2)

    def first_step(rows, code, planes):
        column = columns_of(code)
        e = r.e0[rows, :]
        half1 = near_part(column, e) + sent_part(column, 0, half + own)
        yield
        out = yield from add_up(rows, half1, code, column, 0, vec0)
        r.e1[rows, :] = (e.astype(F32) + out).astype(BF16)

    loop(first_step)
    h = r.h0[middle, :]
    agg = unfold(r.agg_wide[...])
    r.agg0[...] = agg
    delta, saved = node_tail(mm3(h, mats[11]) + mm3(agg, mats[12]), mats[13], mats[14], rows_of(3))
    for j, v in enumerate(saved):
        r.step_kept[j] = v
    h = h + delta
    r.h1[...] = h
    r.hb[middle, :] = 0.5 * mm3(h, mats[16])
    mine = r.hb.at[middle]
    latents = neighbours(2, mine, r.hb.at[pl.ds(0, own)], mine, r.hb.at[pl.ds(2 * own, own)])
    start(latents)
    r.recv_table[...] = side_by_side(0.5 * (mm3(h, mats[17]) + rows_of(4)[0]))
    put_inner(r.hb[middle, :])

    put_weights(1)
    r.agg_wide[...] = jnp.zeros_like(r.agg_wide)
    vec1 = rows_of(4)

    def near_step(rows, code, planes):
        column = columns_of(code)
        half1 = near_part(column, r.e1[rows, :]) + sent_part(column, 0, half)
        yield
        kept[2][2][rows, :], kept[2][3][rows, :] = split(half1)

    def second_step(rows, code, planes):
        column = columns_of(code)
        half1 = kept[2][2][rows, :].astype(F32) + kept[2][3][rows, :].astype(F32)
        half1 = half1 + sent_part(column, half, half + own)
        yield
        yield from add_up(rows, half1, code, column, 1, vec1)

    loop(near_step)
    wait(latents)
    put_outer(r.hb[0:own, :], r.hb[2 * own :, :])
    loop(second_step)

    def slot(group, places, which):
        at = places.index(which) * LAT
        return group.acc.at[pl.ds(at, LAT)]

    def put(group, places, which, value):
        slot(group, places, which)[...] = value

    def put_rows(group, places, at, rows):
        base = len(places) * LAT + at
        for v in rows:
            group.acc[base : base + v.shape[0], :] = v
            base += v.shape[0]
        return base

    def finish_step(group, at):
        for index in range(at, group.steps):
            group.step(index)

    put1, put2, put3, _ = (partial(put, group, places) for group, places in zip(groups, PLACES))
    agg = unfold(r.agg_wide[...])
    h = r.h1[...]
    vec = rows_of(5)
    delta, saved = node_tail(mm3(h, mats[20]) + mm3(agg, mats[21]), mats[22], mats[23], vec)
    out = h + delta
    base = ROWS0 + 30
    s1, d1 = silu_half(0.5 * (mm3(out, mats[4]) + vecs[base : base + 1, :]))
    s2, d2 = silu_half(0.5 * (mm3(s1, mats[5]) + vecs[base + 1 : base + 2, :]))
    ends = vecs[base + 2 : base + 4, :]
    keep = r.keep[...]
    goal = r.goal[...]
    diff = mm3(ends, s2, NT) - goal
    kept_diff = diff * keep
    dpred = 2.0 * kept_diff
    dz2 = mm3(dpred, 0.5 * ends, TN) * d2
    dz1 = mm3(dz2, 0.5 * mats[5], NT) * d1
    d = mm3(dz1, mats[4], NT)
    dz, g_second, g_third, rows = node_tail_back(d, saved, mats[22], mats[23], vec)
    r.dh[...] = d + mm3(dz, mats[20], NT)
    r.dagg[...] = fold_table(mm3(dz, mats[21], NT))
    put1(4, mm3(out, dz1, TN))
    put1(5, mm3(s1, dz2, TN))
    put1(20, mm3(h, dz, TN))
    put1(21, mm3(agg, dz, TN))
    put1(22, g_second)
    put1(23, g_third)
    rows = rows + [row_sum(dz1), row_sum(dz2), mm3(dpred, s2)]
    rows.append(jnp.zeros((7, LAT), F32))
    velocity = r.feat_wide[1, 8:10, :]
    for v in (
        kept_diff * diff,
        velocity * keep,
        velocity * velocity * keep,
        goal * keep,
        goal * goal * keep,
        jnp.broadcast_to(keep, velocity.shape),
    ):
        part = v[:, 0:LAT]
        for j in range(LAT, own, LAT):
            part = part + v[:, j : j + LAT]
        rows.append(part)
    end = put_rows(first, PLACES[0], 0, rows)
    first.acc[end:, :] = jnp.zeros((first.rows - end, LAT), F32)

    def zero(*targets):
        for target in targets:
            target[...] = jnp.zeros_like(target)

    def put_back(step):
        base = 6 + 9 * step
        for i, w in enumerate((mats[base], 0.5 * mats[base + 3], 0.5 * center(mats[base + 4]))):
            r.w[i] = stacked(jnp.transpose(w))

    def chain(rows, column, step, gain, residual):
        recv = recv_of(column)
        d = choose(mm(pick_mask(folded(recv, half), 0, half), r.dagg[...]), recv >= half)
        if residual is not None:
            d = d + residual
        yield
        return (
            yield from edge_tail_back(
                rows, d, kept[1 + step], r.w[1], r.w[2], gain, ones, r.sums
            )
        )

    def add_sent(ref, code, begin, wide):
        ref[...] += mm(add_mask(send_of(code) - begin, ref.shape[0]), wide)

    def add_received(code, column, dz1):
        r.recv_total[...] += mm(
            add_mask(folded(recv_of(code), half), half), halves(dz1, recv_of(column) >= half)
        )

    def slots_of(group, places, step):
        base = 6 + 9 * step
        return [slot(group, places, which) for which in (base, base + 3, base + 4)]

    def add_grads(grads, e, dz1b, dz2b, dcb, s1, s2):
        grads[0][...] += mm(e, dz1b, TN)
        grads[1][...] += mm(s1, dz2b, TN)
        grads[2][...] += mm(s2, dcb, TN)

    put_back(1)
    grads1 = slots_of(second, PLACES[1], 1)
    zero(*grads1, r.sums, r.recv_total, r.inner_total, r.outer_total)
    gain1 = vec1[3]

    def chain_step(rows, code, planes):
        column = columns_of(code)
        dz1, *others = yield from chain(rows, column, 1, gain1, None)
        for ref, v in zip((kept[2][3], kept[2][2], kept[2][0], kept[2][1]), others):
            ref[rows, :] = v
        r.de[rows, :] = dz1.astype(BF16)
        add_sent(r.outer_total, code, half, halves(dz1, upper_of(column)))

    def grads_step(rows, code, planes):
        column = columns_of(code)
        dz1b = r.de[rows, :]
        s1, s2, dcb, dz2b = (ref[rows, :] for ref in kept[2])
        add_grads(grads1, r.e1[rows, :], dz1b, dz2b, dcb, s1, s2)
        dz1 = dz1b.astype(F32)
        add_received(code, column, dz1)
        add_sent(r.inner_total, code, 0, halves(dz1, upper_of(column)))
        r.de[rows, :] = mm(twice(dz1b), r.w[0]).astype(BF16)
        yield

    loop(chain_step, steps_of(first))
    r.spread[0:own, :] = r.outer_total[:, :LAT]
    r.spread[2 * own :, :] = r.outer_total[:, LAT:]
    rims = neighbours(
        4, r.spread.at[pl.ds(2 * own, own)], r.rims.at[0], r.spread.at[pl.ds(0, own)], r.rims.at[1]
    )
    start(rims)
    loop(grads_step)
    grads1[2][...] = center(grads1[2][...])
    end = put_rows(second, PLACES[1], 0, finish_sums(r.sums))
    second.acc[end:, :] = jnp.zeros((second.rows - end, LAT), F32)
    got = unfold(r.recv_total[...])
    h = r.h1[...]
    put2(17, mm3(h, got, TN))
    d = r.dh[...] + mm3(got, mats[17], NT)
    sent = unfold(r.inner_total[...])
    wait(rims)
    finish_step(first, turns)
    sent = sent + r.rims[0] + r.rims[1]
    put2(16, mm3(h, sent, TN))
    d = d + mm3(sent, mats[16], NT)
    saved = [r.step_kept[j] for j in range(4)]
    dz, g_second, g_third, rows = node_tail_back(d, saved, mats[13], mats[14], rows_of(3))
    put2(11, mm3(r.h0[middle, :], dz, TN))
    put2(12, mm3(r.agg0[...], dz, TN))
    put2(13, g_second)
    put2(14, g_third)
    put_rows(third, PLACES[2], 0, rows)
    r.dh[...] = d + mm3(dz, mats[11], NT)
    r.dagg[...] = fold_table(mm3(dz, mats[12], NT))

    put_back(0)
    grads0 = slots_of(third, PLACES[2], 0)
    zero(*grads0, r.sums, r.recv_total, r.inner_total, r.outer_total)
    gain0 = vec0[3]

    def whole_step(rows, code, planes):
        column = columns_of(code)
        de = r.de[rows, :].astype(F32)
        dz1, *others = yield from chain(rows, column, 0, gain0, de)
        dz1b = dz1.astype(BF16)
        yield
        add_grads(grads0, r.e0[rows, :], dz1b, *others)
        wide = halves(dz1, upper_of(column))
        add_sent(r.inner_total, code, 0, wide)
        add_sent(r.outer_total, code, half, wide)
        add_received(code, column, dz1)
        r.de[rows, :] = (de + mm(twice(dz1b), r.w[0])).astype(BF16)

    loop(whole_step, steps_of(second))
    grads0[2][...] = center(grads0[2][...])
    sent = unfold(r.inner_total[...])
    sent = jnp.concatenate([r.outer_total[:, :LAT], sent, r.outer_total[:, LAT:]], 0)
    got = unfold(r.recv_total[...])
    h = r.h0[...]
    put3(7, mm3(h, sent, TN))
    put3(8, mm3(h[own : 2 * own], got, TN))
    d = mm3(sent, mats[7], NT)
    inner = d[own : 2 * own] + r.dh[...] + mm3(got, mats[8], NT)
    d = jnp.concatenate([d[:own], inner, d[2 * own :]], 0)
    saved = [r.node_kept[j] for j in range(4)]
    dz, g_second, g_third, more = node_tail_back(d, saved, mats[0], mats[1], rows_of(0))
    put3(0, g_second)
    put3(1, g_third)
    plain, onehot = particle_inputs()
    rows = finish_sums(r.sums) + more + [mm3(plain, dz), mm3(onehot, dz)]
    end = put_rows(third, PLACES[2], 5, rows)
    third.acc[end:, :] = jnp.zeros((third.rows - end, LAT), F32)
    third.step(0)
    finish_step(second, turns)

    enc_grads = [slot(fourth, PLACES[3], which) for which in PLACES[3]]
    zero(*enc_grads, r.sums, r.we)
    r.w[0] = stacked(jnp.transpose(0.5 * mats[2]))
    r.w[1] = stacked(jnp.transpose(0.5 * center(mats[3])))
    gain = rows_of(1)[3]

    def encoder_back(rows, code, planes):
        d = r.de[rows, :].astype(F32)
        dz1, dz2b, dcb, s1, s2 = yield from edge_tail_back(
            rows, d, kept[0], r.w[0], r.w[1], gain, ones, r.sums
        )
        yield
        enc_grads[0][...] += mm(s1, dz2b, TN)
        enc_grads[1][...] += mm(s2, dcb, TN)
        r.we[...] += mm(features(planes).astype(BF16), dz1.astype(BF16))

    loop(encoder_back, {2: partial(third.step, 1)})
    enc_grads[1][...] = center(enc_grads[1][...])
    end = put_rows(fourth, PLACES[3], 0, finish_sums(r.sums) + [r.we[...]])
    fourth.acc[end:, :] = jnp.zeros((fourth.rows - end, LAT), F32)

    def swap(at, source, target):
        return pltpu.make_async_remote_copy(
            src_ref=source,
            dst_ref=target,
            send_sem=r.pair_send.at[at],
            recv_sem=r.pair_recv.at[at],
            device_id=sibling,
            device_id_type=MESH,
        )

    def gradient(which):
        for group, places in zip(groups, PLACES):
            if which in places:
                return group.full[places.index(which) * LAT : (places.index(which) + 1) * LAT, :]
        return None

    def ranked(which):
        return slice(which * rank, (which + 1) * rank)

    fourth.step(0)
    for group, places, at, size in zip(groups[:2], PLACES, STARTS, ROWS):
        base = len(places) * LAT
        r.small_mine[at : at + size, :] = group.full[base : base + size, :]
    small = swap(0, r.small_mine, r.small_theirs)
    small.start()
    fetches[3].wait()
    for which in range(mats_count):
        r.projected[ranked(which), :] = mm3(r.factors[which], r.errors[which], NT)
    small.wait()
    small = r.small_mine[...] + r.small_theirs[...]
    r.small[0 : STARTS[2], :] = small
    at = 16 + 10
    scale = 1.0 / jnp.sum(small[at : at + 1, :], 1, keepdims=True)

    def take(chosen):
        for which in chosen:
            part = gradient(which)
            r.total[which] = part * scale + r.errors[which]
            r.projected[ranked(which), :] += scale * mm3(r.factors[which], part, NT)

    third.step(2)
    fourth.step(1)
    take(PLACES[0])
    for index in range(3, third.steps):
        third.step(index)
        fourth.step(index - 1)
        if index == 3:
            take(PLACES[1])
    take(PLACES[2])
    finish_step(fourth, third.steps - 1)
    take(PLACES[3])
    end = mats_count * rank
    for group, places, at, size in zip(groups[2:], PLACES[2:], STARTS[2:], ROWS[2:]):
        base = len(places) * LAT
        at = end + at - STARTS[2]
        r.projected[at : at + size, :] = group.full[base : base + size, :]
    both = swap(1, r.projected, r.projected_theirs)
    both.start()
    both.wait()
    r.small[STARTS[2] :, :] = r.projected[end:, :] + r.projected_theirs[end:, :]
    both = (r.projected[0:end, :] + r.projected_theirs[0:end, :]).reshape(mats_count, rank, LAT)
    columns = [both[:, i, :] for i in range(rank)]
    for i in range(rank):
        v = columns[i]
        v = v * lax.rsqrt(jnp.sum(v * v, 1, keepdims=True) + 1e-12)
        columns[i] = v
        for j in range(i + 1, rank):
            columns[j] = columns[j] - jnp.sum(v * columns[j], 1, keepdims=True) * v
    for i in range(rank):
        r.left[:, i, :] = columns[i]
    for which in range(mats_count):
        r.right_mine[ranked(which), :] = mm3(r.left[which], r.total[which])
    both = swap(2, r.right_mine, r.right_theirs)
    both.start()
    both.wait()
    r.right[...] = (r.right_mine[...] + r.right_theirs[...]).reshape(mats_count, rank, LAT)


def train(inputs, count_edge):
    own = inputs["goal"].shape[1]
    lines = inputs["senders"].shape
    count = lines[0] * LAT
    mats_count, rank, _ = inputs["factors"].shape
    reducers = [
        Reducer(count_edge, len(places) * LAT + rows)
        for places, rows in zip(PLACES, ROWS)
    ]
    flat = lambda *dims: pltpu.VMEM(dims, F32)
    half = lambda *dims: pltpu.VMEM(dims, BF16)
    small, late = STARTS[4], STARTS[4] - STARTS[2]
    outs = {
        "total": (mats_count, LAT, LAT),
        "left": (mats_count, rank, LAT),
        "right": (mats_count, rank, LAT),
        "small": (small, LAT),
    }
    scratch = {
        "code": pltpu.VMEM(lines, jnp.int32),
        "mats": flat(*inputs["mats_in"].shape),
        "errors": flat(*inputs["errors_in"].shape),
        "keep": flat(1, own),
        "feat_wide": flat(3, NFEAT + 2, own),
        "w": half(3, 2 * LAT, LAT),
        "h0": flat(3 * own, LAT),
        "node_kept": flat(4, 3 * own, LAT),
        "step_kept": flat(4, own, LAT),
        "senders_table": half(own // 2 + own, 2 * LAT),
        "recv_table": half(own, 2 * LAT),
        "dagg": half(own // 2, 2 * LAT),
        "agg0": flat(own, LAT),
        "h1": flat(own, LAT),
        "hb": flat(3 * own, LAT),
        "dh": flat(own, LAT),
        "rims": flat(2, own, LAT),
        "recv_total": flat(own // 2, 2 * LAT),
        "inner_total": flat(own // 2, 2 * LAT),
        "outer_total": flat(own, 2 * LAT),
        "sums": flat(5, 8, LAT),
        "we": flat(EFEAT, LAT),
        "e0": half(count, LAT),
        "e1": half(count, LAT),
        "de": half(count, LAT),
        "small_mine": flat(STARTS[2], LAT),
        "small_theirs": flat(STARTS[2], LAT),
        "projected": flat(mats_count * rank + late, LAT),
        "projected_theirs": flat(mats_count * rank + late, LAT),
        "right_mine": flat(mats_count * rank, LAT),
        "right_theirs": flat(mats_count * rank, LAT),
        "fetch_sem": pltpu.SemaphoreType.DMA((4,)),
        "halo_send": pltpu.SemaphoreType.DMA((6,)),
        "halo_recv": pltpu.SemaphoreType.DMA((6,)),
        "pair_send": pltpu.SemaphoreType.DMA((3,)),
        "pair_recv": pltpu.SemaphoreType.DMA((3,)),
    }
    for name in ("enc", "one", "two"):
        for i in range(4):
            scratch[f"{name}{i}"] = half(count, LAT)
    for i, reducer in enumerate(reducers):
        for name, shape in reducer.scratch().items():
            scratch[f"sum{i}_{name}"] = shape
    vmem = pl.BlockSpec(memory_space=pltpu.VMEM)
    names = list(inputs) + list(outs) + list(scratch)
    return pl.pallas_call(
        partial(train_kernel, reducers, names, mats_count, rank),
        in_specs=[pl.BlockSpec(memory_space=pl.ANY) if name.endswith("_in") else vmem for name in inputs],
        out_specs=[vmem] * len(outs),
        out_shape=[jax.ShapeDtypeStruct(shape, F32) for shape in outs.values()],
        scratch_shapes=list(scratch.values()),
        compiler_params=pltpu.CompilerParams(
            collective_id=0, has_side_effects=True, vmem_limit_bytes=VMEM_LIMIT
        ),
    )(*inputs.values())


VMEM_LIMIT = 62 << 20


def finish_kernel(total, left, right, small, mats, momentum, vecs, vecs_momentum, *outs):
    new_mats, new_momentum, new_errors, new_factors, *outs = outs
    new_vecs, new_vecs_momentum, loss, kept_count, stats = outs
    new_factors[...] = right[...]
    for k in range(total.shape[0]):
        approx = mm3(left[k], right[k], TN)
        moved = 0.9 * momentum[k] + approx
        new_momentum[k] = moved
        new_mats[k] = mats[k] - 4.0 * moved
        new_errors[k] = total[k] - approx

    @pl.when(pl.program_id(0) == 0)
    def _():
        sums = jnp.sum(small[16:28, :], 1, keepdims=True)
        kept = sums[10:11]
        scale = 1.0 / kept
        loss[...] = sums[0:1] + sums[1:2]
        kept_count[...] = kept
        lanes = lax.broadcasted_iota(jnp.int32, stats.shape, 1)
        table = jnp.zeros(stats.shape, F32)
        for i in range(4):
            table = jnp.where(lanes == i, sums[2 + 2 * i : 4 + 2 * i], table)
        stats[...] = table * scale
        n1, e1, n0, enc, _ = STARTS
        cuts = (
            (n0 + 15, 23), (enc + 5, 3), (n0 + 10, 5), (enc, 5), (n0 + 5, 5), (n0, 5), (e1, 5),
            (n1, 9),
        )
        grads = jnp.concatenate([small[at : at + length, :] for at, length in cuts], 0)
        moved = 0.9 * vecs_momentum[...] + grads * scale
        new_vecs_momentum[...] = moved
        new_vecs[...] = vecs[...] - 4.0 * moved


def finish(total, left, right, small, mats, momentum, vecs, vecs_momentum):
    group = 6
    big = pl.BlockSpec((group, LAT, LAT), lambda i: (i, 0, 0))
    thin = pl.BlockSpec((group,) + left.shape[1:], lambda i: (i, 0, 0))
    whole = lambda shape: pl.BlockSpec(shape, lambda i: (0,) * len(shape))
    shape = lambda *dims: jax.ShapeDtypeStruct(dims, F32)
    return pl.pallas_call(
        finish_kernel,
        grid=(total.shape[0] // group,),
        in_specs=[big, thin, thin, whole(small.shape), big, big]
        + [whole(vecs.shape), whole(vecs.shape)],
        out_specs=[big] * 3 + [thin] + [whole(vecs.shape)] * 2 + [whole((1, 1))] * 2 + [whole((2, 4))],
        out_shape=[shape(*total.shape)] * 3
        + [shape(*right.shape)]
        + [shape(*vecs.shape)] * 2
        + [shape(1, 1), shape(1, 1), shape(2, 4)],
    )(total, left, right, small, mats, momentum, vecs, vecs_momentum)


def shards(
    node_feat, node_types, boundary, target, edge_feat, senders, receivers, edge_counts, mats, vecs,
    mats_momentum, vecs_momentum, factors, errors,
):
    own = node_feat.shape[1]
    count = senders.shape[1]
    lines = (count // LAT, LAT)
    few = (own // LAT, LAT)
    inputs = {
        "senders": senders.reshape(lines),
        "receivers": receivers.reshape(lines),
        "counts": edge_counts,
        "x": jnp.transpose(edge_feat, (2, 0, 1)).reshape(EFEAT * lines[0], LAT),
        "node_lines": jnp.transpose(node_feat, (2, 0, 1)).reshape(NFEAT * few[0], LAT),
        "types": node_types.reshape(few),
        "boundary": boundary.reshape(few),
        "goal": target[0].T,
        "mats_in": mats,
        "vecs": vecs,
        "factors": jnp.swapaxes(factors, 1, 2),
        "errors_in": errors[0],
    }
    total, left, right, small = train(inputs, lax.axis_size("edge"))
    new_mats, mats_mom, new_errors, new_factors, new_vecs, vecs_mom, loss, kept, stats = finish(
        total, left, right, small, mats, mats_momentum, vecs, vecs_momentum
    )
    return (
        loss.reshape(()),
        kept.reshape(()),
        stats.T,
        new_mats,
        mats_mom,
        jnp.swapaxes(new_factors, 1, 2),
        new_errors[None],
        new_vecs,
        vecs_mom,
    )


def solution(mesh):
    placed = (
        P("rep", "edge", None),
        P("rep", "edge"),
        P("rep", "edge"),
        P("rep", "edge", None),
        P("rep", "edge", None),
        P("rep", "edge"),
        P("rep", "edge"),
        P("rep", "edge"),
        P(),
        P(),
        P(),
        P(),
        P(),
        P("rep", None, None, None),
    )
    return jax.shard_map(
        shards,
        mesh=mesh,
        in_specs=placed,
        out_specs=(P(), P(), P(), P(), P(), P(), P("rep", None, None, None), P(), P()),
        check_vma=False,
    )
```

profile of v0, /device:TPU:0, one launch (start us, length us, event | category | flops | bytes accessed | tf_op | source)
XLA Modules:
  0.0 147.6 jit_solution(1610199394427146310)
XLA Ops:
  1.3 140.3 %shard_map.205 = (f32[24,128,128]{2,1,0:T(8,128)}, f32[24,8,128]{2,1,0:T(8,128)}, f32[24,8,128]{2,1,0:T(8,128)}, f32[96,128]{1,0:T(8,128)}) custom-call(s32[64,128]{1,0:T(8,128)} %bitcast.23, s32[64,128]{1,0:T(8,128)} %bitcast.24, s32[1,1]{1,0:T(1,128)S(6)} %copy.23.refs_2_, f32[192,128]{1,0:T(8,128)} %bitcast.21, f32[56,128]{1,0:T(8,128)} %bitcast.25, ...), custom_call_target="tpu_custom_call" | custom-call | tf_op jit(solution)/shard_map/pallas_call | solution.py:979
  141.6 5.9 %shard_map.206 = (f32[24,128,128]{2,1,0:T(8,128)}, f32[24,128,128]{2,1,0:T(8,128)}, f32[24,128,128]{2,1,0:T(8,128)}, f32[24,8,128]{2,1,0:T(8,128)}, f32[60,128]{...) custom-call(f32[24,128,128]{2,1,0:T(8,128)} %get-tuple-element.22.total, ...), custom_call_target="tpu_custom_call" | custom-call | tf_op jit(solution)/shard_map/pallas_call | solution.py:1034
where the time goes:
time: 148 us
  Pallas kernels  146 us (99%)
  between operations  1.48 us (1%)
    pallas_call x1, Pallas kernels, train(): pl.pallas_call(partial(train_kernel, reducers, names, mats_count, rank),...  140 us
    pallas_call x1, Pallas kernels, finish(): pl.pallas_call(finish_kernel, grid=(total.shape[0] // group,), in_specs=[...  5.86 us

commit v1 on v0

--- a/solution.py
+++ b/solution.py
@@ -128,7 +128,7 @@
     return dz1, mm3(s1, dz2, TN), mm3(s2, dz3, TN), rows
 
 
-def edge_tail(rows, half, kept, second, third, vec, ones):
+def edge_tail(rows, half, kept, second, third, vec):
     _, b2, b3, g, o = vec
     kept[0][rows, :] = half.astype(BF16)
     s1 = silu_half(half)[0].astype(BF16)
@@ -138,18 +138,18 @@
     s2 = silu_half(half)[0].astype(BF16)
     c = mm(twice(s2), third) + center(b3)
     yield
-    inv = lax.rsqrt(mm((c * c).astype(BF16), ones) + 1e-05)
+    inv = lax.rsqrt(mean_last(c * c) + 1e-05)
     xhat = c * inv
     kept[2][rows, :] = xhat.astype(BF16)
-    kept[3][rows, :] = inv.astype(BF16)
+    kept[3][rows, :] = jnp.broadcast_to(inv, c.shape).astype(BF16)
     return xhat * g + o
 
 
-def edge_tail_back(rows, d, kept, second, third, g, ones, sums):
+def edge_tail_back(rows, d, kept, second, third, g, sums):
     xhat = kept[2][rows, :].astype(F32)
     inv = kept[3][rows, :].astype(F32)
     dx = d * xhat
-    dc = inv * (d * g - xhat * mm((dx * g).astype(BF16), ones))
+    dc = inv * (d * g - xhat * mean_last(dx * g))
     dcb = dc.astype(BF16)
     for at, v in ((2, dc), (3, dx), (4, d)):
         sums[at] += fold_rows(v)
@@ -399,7 +399,6 @@
     for one in fetches:
         one.start()
     mats, vecs = r.mats, r.vecs
-    ones = jnp.full((LAT, LAT), 1.0 / LAT, BF16)
     middle = pl.ds(own, own)
     r["spread"] = r.hb
     r["agg_wide"] = r.recv_total
@@ -474,8 +473,12 @@
 
     turns = count // BLOCK
 
-    def steps_of(group):
-        return {index: partial(group.step, index) for index in range(turns)}
+    def slot_of(group, index):
+        def run():
+            for at in range(index, group.steps if index == 4 else index + 1):
+                group.step(at)
+
+        return run
 
     def loop(body, hooks=None):
         def step(i, unused):
@@ -513,7 +516,7 @@
     def encode(rows, code, planes):
         half = mm3(features(planes), 0.5 * vecs[LEAD:ROWS0, :], TN) + 0.5 * vec[0]
         yield
-        out = yield from edge_tail(rows, half, kept[0], r.w[0], r.w[1], vec, ones)
+        out = yield from edge_tail(rows, half, kept[0], r.w[0], r.w[1], vec)
         r.e0[rows, :] = out.astype(BF16)
 
     loop(encode, {turns // 2: begin})
@@ -561,7 +564,7 @@
         return choose(wide, upper_of(column))
 
     def add_up(rows, half1, code, column, step, vec):
-        out = yield from edge_tail(rows, half1, kept[1 + step], r.w[1], r.w[2], vec, ones)
+        out = yield from edge_tail(rows, half1, kept[1 + step], r.w[1], r.w[2], vec)
         r.agg_wide[...] += mm(
             add_mask(folded(recv_of(code), half), half), halves(out, recv_of(column) >= half)
         )
@@ -697,7 +700,7 @@
         yield
         return (
             yield from edge_tail_back(
-                rows, d, kept[1 + step], r.w[1], r.w[2], gain, ones, r.sums
+                rows, d, kept[1 + step], r.w[1], r.w[2], gain, r.sums
             )
         )
 
@@ -742,7 +745,7 @@
         r.de[rows, :] = mm(twice(dz1b), r.w[0]).astype(BF16)
         yield
 
-    loop(chain_step, steps_of(first))
+    loop(chain_step, {0: slot_of(first, 0), 2: slot_of(first, 1), 3: slot_of(first, 2)})
     r.spread[0:own, :] = r.outer_total[:, :LAT]
     r.spread[2 * own :, :] = r.outer_total[:, LAT:]
     rims = neighbours(
@@ -759,7 +762,7 @@
     d = r.dh[...] + mm3(got, mats[17], NT)
     sent = unfold(r.inner_total[...])
     wait(rims)
-    finish_step(first, turns)
+    first.step(3)
     sent = sent + r.rims[0] + r.rims[1]
     put2(16, mm3(h, sent, TN))
     d = d + mm3(sent, mats[16], NT)
@@ -791,7 +794,9 @@
         add_received(code, column, dz1)
         r.de[rows, :] = (de + mm(twice(dz1b), r.w[0])).astype(BF16)
 
-    loop(whole_step, steps_of(second))
+    hooks = [slot_of(second, 0), slot_of(first, 4), slot_of(second, 1), slot_of(second, 2)]
+    loop(whole_step, dict(enumerate(hooks)))
+    second.step(3)
     grads0[2][...] = center(grads0[2][...])
     sent = unfold(r.inner_total[...])
     sent = jnp.concatenate([r.outer_total[:, :LAT], sent, r.outer_total[:, LAT:]], 0)
@@ -811,7 +816,6 @@
     end = put_rows(third, PLACES[2], 5, rows)
     third.acc[end:, :] = jnp.zeros((third.rows - end, LAT), F32)
     third.step(0)
-    finish_step(second, turns)
 
     enc_grads = [slot(fourth, PLACES[3], which) for which in PLACES[3]]
     zero(*enc_grads, r.sums, r.we)
@@ -822,14 +826,14 @@
     def encoder_back(rows, code, planes):
         d = r.de[rows, :].astype(F32)
         dz1, dz2b, dcb, s1, s2 = yield from edge_tail_back(
-            rows, d, kept[0], r.w[0], r.w[1], gain, ones, r.sums
+            rows, d, kept[0], r.w[0], r.w[1], gain, r.sums
         )
         yield
         enc_grads[0][...] += mm(s1, dz2b, TN)
         enc_grads[1][...] += mm(s2, dcb, TN)
         r.we[...] += mm(features(planes).astype(BF16), dz1.astype(BF16))
 
-    loop(encoder_back, {2: partial(third.step, 1)})
+    loop(encoder_back, {2: slot_of(second, 4), 3: slot_of(third, 1)})
     enc_grads[1][...] = center(enc_grads[1][...])
     end = put_rows(fourth, PLACES[3], 0, finish_sums(r.sums) + [r.we[...]])
     fourth.acc[end:, :] = jnp.zeros((fourth.rows - end, LAT), F32)
@@ -1026,7 +1030,7 @@
 
 
 def finish(total, left, right, small, mats, momentum, vecs, vecs_momentum):
-    group = 6
+    group = 12
     big = pl.BlockSpec((group, LAT, LAT), lambda i: (i, 0, 0))
     thin = pl.BlockSpec((group,) + left.shape[1:], lambda i: (i, 0, 0))
     whole = lambda shape: pl.BlockSpec(shape, lambda i: (0,) * len(shape))

time: 148 us -> 141 us (0.953)
  Pallas kernels: 146 us -> 140 us
    pallas_call x1, Pallas kernels: 140 us -> 135 us  [train(): pl.pallas_call(partial(train_kernel, reducers, names, mats_count, rank),...]
where the time goes in v1:
time: 141 us
  Pallas kernels  140 us (99%)
  between operations  1.48 us (1%)
    pallas_call x1, Pallas kernels, train(): pl.pallas_call(partial(train_kernel, reducers, names, mats_count, rank),...  135 us
    pallas_call x1, Pallas kernels, finish(): pl.pallas_call(finish_kernel, grid=(total.shape[0] // group,), in_specs=[...  4.79 us

profile of v1, /device:TPU:0, one launch (start us, length us, event | category | flops | bytes accessed | tf_op | source)
XLA Modules:
  0.0 141.1 jit_solution(11802274012626634338)
XLA Ops:
  1.3 134.9 %shard_map.205 = (f32[24,128,128]{2,1,0:T(8,128)}, f32[24,8,128]{2,1,0:T(8,128)}, f32[24,8,128]{2,1,0:T(8,128)}, f32[96,128]{1,0:T(8,128)}) custom-call(s32[64,128]{1,0:T(8,128)} %bitcast.23, s32[64,128]{1,0:T(8,128)} %bitcast.24, s32[1,1]{1,0:T(1,128)S(6)} %copy.23.refs_2_, f32[192,128]{1,0:T(8,128)} %bitcast.21, f32[56,128]{1,0:T(8,128)} %bitcast.25, ...), custom_call_target="tpu_custom_call" | custom-call | tf_op jit(solution)/shard_map/pallas_call | solution.py:983
  136.2 4.8 %shard_map.206 = (f32[24,128,128]{2,1,0:T(8,128)}, f32[24,128,128]{2,1,0:T(8,128)}, f32[24,128,128]{2,1,0:T(8,128)}, f32[24,8,128]{2,1,0:T(8,128)}, f32[60,128]{...) custom-call(f32[24,128,128]{2,1,0:T(8,128)} %get-tuple-element.22.total, ...), custom_call_target="tpu_custom_call" | custom-call | tf_op jit(solution)/shard_map/pallas_call | solution.py:1038
